TPU v7x, 512 devices: a whole 4x8x8 slice. The times are simulated.
512 devices in a mesh: section: 16 (over y, core), tm: 32 (over x, z).
Axes of the slice: x: 4, y: 8, z: 8, core: 2. Of those that a mesh axis runs over, the one named last changes fastest.
Arguments:
- clips: bfloat16 [2, 32, 16, 8, 128], P(None, 'tm'), may hold values from -6 to 6
- kernels: bfloat16 [16, 3, 3, 3, 128, 128], P('section'), may hold values from -0.078125 to 0.078125
- cotangent: bfloat16 [2, 32, 16, 8, 128], P(None, 'tm'), may hold values from -6 to 6
Outputs:
- activations: bfloat16 [16, 2, 32, 16, 8, 128], P('section', None, 'tm')
- input_grads: bfloat16 [16, 2, 32, 16, 8, 128], P('section', None, 'tm')
- kernel_grads: float32 [16, 3, 3, 3, 128, 128], P('section')
All inputs are finite; a program needn't handle non-finite values.
Results may differ from a plain program's by a relative error of at most 0.035.
Values may be sent and summed in bfloat16 or wider, within the bound.
A program may use at most 64 MiB of HBM per device.

v0:
```python
import jax
import jax.numpy as jnp
from jax import lax
from jax.sharding import PartitionSpec as P


def shifted(value, axis, steps):
    count = lax.axis_size(axis)
    initial, last = (max(0, -steps), min(count, count - steps))
    return lax.ppermute(value, axis, [(source, source + steps) for source in range(initial, last)])


def for_sending(shard):
    return jax.tree.map(lambda a: a.astype(jnp.bfloat16) if a.dtype == jnp.float32 else a, shard)


def conv_time(values, kernel, front, back):
    return lax.conv_general_dilated(
        values[None],
        kernel,
        (1, 1, 1),
        [(front, back), (1, 1), (1, 1)],
        dimension_numbers=("NDHWC", "DHWIO", "NDHWC"),
        preferred_element_type=jnp.float32,
    )[0]


def kernel_terms(silu_ext, grad_out):
    height = grad_out.shape[1]
    width = grad_out.shape[2]
    chan = grad_out.shape[3]
    padded = jnp.pad(silu_ext, ((0, 0), (1, 1), (1, 1), (0, 0)))
    flat_grad = grad_out.reshape(height * width, chan)
    layers = []
    for step_t in range(3):
        pieces = []
        for step_h in range(3):
            for step_w in range(3):
                pieces.append(padded[step_t, step_h : step_h + height, step_w : step_w + width, :])
        patches = jnp.stack(pieces, axis=2).reshape(height * width, 9 * chan)
        total = lax.dot_general(
            patches, flat_grad, (((0,), (0,)), ((), ())), preferred_element_type=jnp.float32
        )
        layers.append(total.reshape(3, 3, chan, chan))
    return jnp.stack(layers)


def store_slot(buffer, update, slot, live):
    previous = lax.dynamic_index_in_dim(buffer, slot, 0, keepdims=False)
    return lax.dynamic_update_index_in_dim(buffer, jnp.where(live, update, previous), slot, 0)


def body(clips, kernels, cotangent):
    sections = lax.axis_size("section")
    section_index = lax.axis_index("section")
    micro, frames, height, width, chan = clips.shape
    kernel = kernels[0]
    flipped = jnp.swapaxes(kernel[::-1, ::-1, ::-1], 3, 4)
    ticks = micro + sections - 1
    norm = 1.0 / jnp.sqrt(jnp.float32(micro * frames * lax.axis_size("tm") * height * width))

    def block_fwd(values, rim_frames):
        extended = jnp.concatenate([rim_frames, values], axis=0)
        silu_ext = jax.nn.silu(extended.astype(jnp.float32)).astype(jnp.bfloat16)
        return (values.astype(jnp.float32) + conv_time(silu_ext, kernel, 0, 0)).astype(jnp.bfloat16)

    def fwd_tick(tick, carry):
        incoming, acts, saved, rims = carry
        which = tick - section_index
        live = jnp.logical_and(which >= 0, which < micro)
        slot = jnp.clip(which, 0, micro - 1)
        first = lax.dynamic_index_in_dim(
            clips, jnp.clip(tick, 0, micro - 1).astype(jnp.int32), 0, keepdims=False
        )
        values = jnp.where(section_index == 0, first, incoming)
        earlier = []
        moving = values
        for hop in range(2):
            moving = shifted(moving, "tm", 1)
            earlier.append(moving)
        rim_frames = jnp.concatenate([earlier[1], earlier[0]], axis=0)
        result = lax.cond(
            live, block_fwd, lambda vals, rimv: jnp.zeros_like(vals), values, rim_frames
        )
        acts = store_slot(acts, result, slot, live)
        saved = store_slot(saved, values, slot, live)
        rims = store_slot(rims, rim_frames, slot, live)
        incoming = shifted(result, "section", 1)
        return (incoming, acts, saved, rims)

    start = (
        jnp.zeros_like(clips[0]),
        jnp.zeros_like(clips),
        jnp.zeros_like(clips),
        jnp.zeros((micro, 2, height, width, chan), clips.dtype),
    )
    _, acts, saved, rims = lax.fori_loop(0, ticks, fwd_tick, start)
    zero_kernel = jnp.zeros((3, 3, 3, chan, chan), jnp.float32)

    def bwd_tick(tick, carry):
        incoming, grads, kacc = carry
        which = tick - (sections - 1 - section_index)
        live = jnp.logical_and(which >= 0, which < micro)
        slot = jnp.clip(which, 0, micro - 1)
        last = lax.dynamic_index_in_dim(
            cotangent, jnp.clip(tick, 0, micro - 1).astype(jnp.int32), 0, keepdims=False
        )
        grad_out = jnp.where(section_index == sections - 1, last, incoming)
        values = lax.dynamic_index_in_dim(saved, slot, 0, keepdims=False)
        rim_frames = lax.dynamic_index_in_dim(rims, slot, 0, keepdims=False)
        silu_ext = jax.nn.silu(
            jnp.concatenate([rim_frames, values], axis=0).astype(jnp.float32)
        ).astype(jnp.bfloat16)

        def work_part(grads_in, silu_in):
            return (conv_time(grads_in, flipped, 2, 2), kernel_terms(silu_in, grads_in))

        def spare_part(grads_in, silu_in):
            return (jnp.zeros((3, height, width, chan), jnp.float32), zero_kernel)

        back_ext, kterm = lax.cond(live, work_part, spare_part, grad_out, silu_ext)
        back_vals = back_ext[0:1]
        for hop in range(2):
            back_vals = (
                jax.tree.map(
                    lambda part, own: part.astype(own.dtype),
                    shifted(for_sending(back_vals), "tm", -1),
                    back_vals,
                )
                + back_ext[hop + 1 : hop + 2]
            )
        floats = values.astype(jnp.float32)
        logistic = jax.nn.sigmoid(floats)
        deriv = logistic * (1.0 + floats * (1.0 - logistic))
        input_grad = (grad_out.astype(jnp.float32) + back_vals * deriv).astype(jnp.bfloat16)
        grads = store_slot(grads, input_grad, slot, live)
        kacc = kacc + kterm
        incoming = shifted(input_grad, "section", -1)
        return (incoming, grads, kacc)

    start_back = (jnp.zeros_like(clips[0]), jnp.zeros_like(clips), zero_kernel)
    _, grads, kacc = lax.fori_loop(0, ticks, bwd_tick, start_back)
    summed = lax.psum(kacc.astype(jnp.bfloat16), "tm").astype(jnp.float32) * norm
    return (acts[None], grads[None], summed[None])


def solution(mesh):
    placed = (
        P(None, "tm", None, None, None),
        P("section", None, None, None, None, None),
        P(None, "tm", None, None, None),
    )
    return jax.shard_map(
        body,
        mesh=mesh,
        in_specs=placed,
        out_specs=(
            P("section", None, "tm", None, None, None),
            P("section", None, "tm", None, None, None),
            P("section", None, None, None, None, None),
        ),
        check_vma=False,
    )
```

profile of v0, /device:TPU:1, one launch (start us, length us, event | category | flops | bytes accessed | tf_op | source)
XLA Modules:
  0.0 1130.9 jit_solution(3226930125482872030)
XLA Ops:
  11.7 379.4 %while.40 = (s32[]{:T(128)}, bf16[1,16,8,128]{3,2,1,0:T(8,128)(2,1)S(1)}, bf16[2,1,16,8,128]{4,3,2,1,0:T(8,128)(2,1)S(1)}, bf16[2,1,16,8,128]{4,3,2,1,0:T(8,128)...) while((s32[]{:T(128)}, ...), condition=%wide.region_3.4_spmd, body=%wide.region_0.3_spmd.sunk | while | flops 100122632 | bytes 2491262 | solution.py:97
  24.7 5.5 collective-permute-start.2
  67.4 5.4 collective-permute-start.2
  88.9 6.3 collective-permute-start.2
  111.2 5.4 collective-permute-start.2
  126.4 5.2 collective-permute-start.1
  132.6 5.4 collective-permute-start.2
  154.1 5.4 collective-permute-start.2
  175.5 5.4 collective-permute-start.2
  197.0 5.4 collective-permute-start.2
  206.1 5.3 collective-permute-start
  212.4 6.1 collective-permute-start.1
  219.5 5.4 collective-permute-start.2
  228.6 6.0 collective-permute-start
  235.6 6.1 collective-permute-start.1
  242.7 5.4 collective-permute-start.2
  251.8 6.0 collective-permute-start
  258.9 6.1 collective-permute-start.1
  266.0 5.4 collective-permute-start.2
  275.1 6.0 collective-permute-start
  282.1 6.1 collective-permute-start.1
  289.2 5.6 collective-permute-start.2
  298.5 6.0 collective-permute-start
  305.5 6.1 collective-permute-start.1
  312.6 5.4 collective-permute-start.2
  321.7 5.9 collective-permute-start
  328.6 6.1 collective-permute-start.1
  335.7 5.4 collective-permute-start.2
  344.8 6.2 collective-permute-start
  352.0 5.9 collective-permute-start.1
  358.9 6.1 collective-permute-start.2
  368.8 5.7 collective-permute-start
  375.5 5.8 collective-permute-start.1
  382.3 7.2 collective-permute-start.2
  392.3 561.3 %while.41 = (s32[]{:T(128)}, bf16[1,16,8,128]{3,2,1,0:T(8,128)(2,1)}, bf16[2,1,16,8,128]{4,3,2,1,0:T(8,128)(2,1)}, f32[3,3,3,128,128]{4,3,2,1,0:T(8,128)S(1)}, p...) while((s32[]{:T(128)}, ...), condition=%wide.region_7.8_spmd.clone, body=%wide.region_4.7_spmd.clone.sunk | while | flops 215154704 | bytes 24117732 | solution.py:142
  398.4 5.8 collective-permute-done.3
  417.1 6.6 collective-permute-done.5
  429.8 5.8 collective-permute-done.3
  448.4 5.7 collective-permute-done.5
  460.2 5.8 collective-permute-done.3
  478.9 6.6 collective-permute-done.5
  491.6 5.8 collective-permute-done.3
  510.3 5.7 collective-permute-done.5
  522.0 5.5 collective-permute-done.3
  540.4 6.0 collective-permute-done.5
  552.5 5.5 collective-permute-done.3
  570.8 5.7 collective-permute-done.5
  582.6 5.5 collective-permute-done.3
  601.0 6.0 collective-permute-done.5
  613.1 5.5 collective-permute-done.3
  641.5 5.5 collective-permute-done.3
  669.8 5.5 collective-permute-done.3
  698.2 5.5 collective-permute-done.3
  726.6 5.5 collective-permute-done.3
  754.9 5.5 collective-permute-done.3
  783.3 5.5 collective-permute-done.3
  801.6 53.7 %collective-permute-done.5 = bf16[1,16,8,128]{3,2,1,0:T(8,128)(2,1)} collective-permute-done((bf16[1,16,8,128]{3,2,1,0:T(8,128)(2,1)}, bf16[1,16,8,128]{3,2,1,0:T(8,128)(2,1)}, u32[]{:S(2)}, u32[]{:S(2)}) %collective-permute-start.5) | collective-permute-done | bytes 32800 | tf_op jit(solution)/shard_map/while/body/eval_jaxpr/ppermute | solution.py:10
  858.5 6.8 conditional.6
  867.4 5.5 collective-permute-done.3
  892.7 6.8 conditional.6
  901.7 5.5 collective-permute-done.3
  929.1 5.8 collective-permute-done.3
  944.9 7.5 collective-permute-start.5
  954.7 166.8 %all-reduce.3.cloned.1.call-done = bf16[3,3,3,128,128]{4,3,2,1,0:T(8,128)(2,1)} async-done(((bf16[3,3,3,128,128]{4,3,2,1,0:T(8,128)(2,1)}), bf16[3,3,3,128,128]{4,3,2,1,0:T(8,128)(2,1)}) %all-reduce.3.cloned.1.call-update) | async-done | bytes 884752 | tf_op jit(solution)/shard_map/psum | solution.py:143
  (584 shorter events, 574.4 us)
Async XLA Ops:
  7.2 1114.4 %all-reduce.3.cloned.1.call-start = ((), (), s32[]{:S(2)}) async-start(), calls=%async_computation | async-start | bytes 1769472 | tf_op jit(solution)/shard_map/psum | solution.py:143
  24.7 7.6 collective-permute-start.2
  67.4 6.9 collective-permute-start.2
  88.9 7.8 collective-permute-start.2
  111.2 6.9 collective-permute-start.2
  132.6 6.9 collective-permute-start.2
  154.1 6.9 collective-permute-start.2
  175.5 6.9 collective-permute-start.2
  197.0 6.9 collective-permute-start.2
  212.4 7.1 collective-permute-start.1
  219.5 6.9 collective-permute-start.2
  228.6 7.1 collective-permute-start
  235.6 7.1 collective-permute-start.1
  242.7 6.9 collective-permute-start.2
  251.8 7.1 collective-permute-start
  258.9 7.1 collective-permute-start.1
  266.0 6.9 collective-permute-start.2
  275.1 7.1 collective-permute-start
  282.1 7.1 collective-permute-start.1
  289.2 7.1 collective-permute-start.2
  298.5 7.1 collective-permute-start
  305.5 7.1 collective-permute-start.1
  312.6 7.0 collective-permute-start.2
  321.7 6.9 collective-permute-start
  328.6 7.1 collective-permute-start.1
  335.7 6.9 collective-permute-start.2
  344.8 7.2 collective-permute-start
  352.0 6.9 collective-permute-start.1
  358.9 7.7 collective-permute-start.2
  375.5 6.8 collective-permute-start.1
  382.3 8.7 collective-permute-start.2
  397.1 7.0 collective-permute-start.3
  405.6 7.4 collective-permute-start.4
  414.5 9.1 collective-permute-start.5
  428.5 7.0 collective-permute-start.3
  437.0 7.4 collective-permute-start.4
  445.9 8.2 collective-permute-start.5
  458.9 7.0 collective-permute-start.3
  467.5 7.4 collective-permute-start.4
  476.4 9.1 collective-permute-start.5
  490.3 7.0 collective-permute-start.3
  498.8 7.4 collective-permute-start.4
  507.7 8.2 collective-permute-start.5
  529.0 7.4 collective-permute-start.4
  537.9 8.5 collective-permute-start.5
  559.4 7.4 collective-permute-start.4
  568.3 8.2 collective-permute-start.5
  589.6 7.4 collective-permute-start.4
  598.4 8.5 collective-permute-start.5
  620.0 7.4 collective-permute-start.4
  648.4 7.4 collective-permute-start.4
  676.8 7.4 collective-permute-start.4
  705.1 7.4 collective-permute-start.4
  733.5 7.4 collective-permute-start.4
  761.9 7.4 collective-permute-start.4
  790.2 7.4 collective-permute-start.4
  799.1 56.3 %collective-permute-start.5 = (bf16[1,16,8,128]{3,2,1,0:T(8,128)(2,1)}, bf16[1,16,8,128]{3,2,1,0:T(8,128)(2,1)}, u32[]{:S(2)}, u32[]{:S(2)}) collective-permute-start(bf16[1,16,8,128]{3,2,1,0:T(8,128)(2,1)} %get-tuple-element.664), channel_id=1, source_target_pairs={{32,0},{64,32},{96,64},{128,96},{160,128},{192,160},{224,192},{256... | collective-permute-start | bytes 98312 | tf_op jit(solution)/shard_map/while/body/eval_jaxpr/ppermute | solution.py:10
  866.1 6.8 collective-permute-start.3
  874.3 7.4 collective-permute-start.4
  900.4 6.8 collective-permute-start.3
  908.6 7.4 collective-permute-start.4
  927.8 7.0 collective-permute-start.3
  936.3 7.1 collective-permute-start.4
  944.9 8.6 collective-permute-start.5
  (47 other events, 258.6 us)
Sparse Core Ops, SparseCore 0:
  954.8 166.6 all-reduce.2
where the time goes:
time: 1150 us; the launch traced here: 1130 us
  waiting for transfers between devices  502 us (44%)
  starting transfers between devices  361 us (31%)
  other arithmetic  142 us (12%)
  local copies, waits for them, and re-layouts  99.8 us (9%)
  between operations  14.1 us (1%)
    ppermute x102, starting transfers between devices, shifted(): lax.ppermute(value, axis, [(source, source + steps) for source in range(i...  361 us
    ppermute x102, waiting for transfers between devices, shifted(): lax.ppermute(value, axis, [(source, source + steps) for source in range(i...  336 us
    psum x1, waiting for transfers between devices, body(): lax.psum(kacc.astype(jnp.bfloat16), 'tm').astype(jnp.float32) * norm  167 us
    dynamic_update_slice x68, other arithmetic, store_slot(): lax.dynamic_update_index_in_dim(buffer, jnp.where(live, update, previous)...  75.2 us
    dynamic_slice x51, local copies, waits for them, and re-layouts, store_slot(): previous = lax.dynamic_index_in_dim(buffer, slot, 0, keepdims=False)  36.7 us
    convert_element_type x17, other arithmetic, for_sending(): a.astype(jnp.bfloat16)  24.9 us
    select_n x17, other arithmetic, bwd_tick(): grad_out = jnp.where(section_index == sections - 1, last, incoming)  23.8 us
  transfers between devices with their start and end apart: 103, of which 87 were waited for; matrix products, arithmetic and copies ran while one was open for 5% of the time, Pallas kernels for 0%

commit v1 on v0

v1 whole, which is shorter than its diff:
```python
import functools

import jax
import jax.numpy as jnp
from jax import lax
from jax.experimental import pallas as pl
from jax.experimental.pallas import tpu as pltpu
from jax.sharding import PartitionSpec as P

MESH = pl.DeviceIdType.MESH
PLANES = 8
ROWS = 112
BF16 = jnp.bfloat16
F32 = jnp.float32


def silu(v):
    return v / (1.0 + jnp.exp(-v))


def silu_slope(v):
    sig = 1.0 / (1.0 + jnp.exp(-v))
    return sig * (1.0 + v * (1.0 - sig))


def shift_w(a, d):
    r = pltpu.roll(a, (-d) % 8, 1)
    w = lax.broadcasted_iota(jnp.int32, a.shape, 1)
    return jnp.where(w < 7, r, 0.0) if d == 1 else jnp.where(w > 0, r, 0.0)


def shift_h(a, d):
    z = jnp.zeros((1,) + a.shape[1:], a.dtype)
    return jnp.concatenate([a[1:], z], axis=0) if d == 1 else jnp.concatenate([z, a[:-1]], axis=0)


def conv(frames, weight):
    count = len(frames) - 2
    rows = [jnp.concatenate(frames[f : f + 3], axis=1) for f in range(count)]
    left = jnp.concatenate(rows, axis=0) if count > 1 else rows[0]
    full = jnp.dot(left, weight[...], preferred_element_type=F32)
    outs = []
    for f in range(count):
        part = full[f * 128 : (f + 1) * 128]
        cols = []
        for dw in range(3):
            g = [part[:, (dh * 3 + dw) * 128 : (dh * 3 + dw + 1) * 128].reshape(16, 8, 128) for dh in range(3)]
            cols.append(g[1] + shift_h(g[0], -1) + shift_h(g[2], 1))
        acc = cols[1] + shift_w(cols[0], -1) + shift_w(cols[2], 1)
        outs.append(acc.reshape(128, 128))
    return outs


def tm_of(m, j):
    x = j // 4
    a = j % 4
    return x * 8 + 4 * m + a + (x % 2) * (3 - 2 * a)


def kernel(
    clips, k_ref, cot, act, grad, kg,
    X0, X1, X2, G2, G1, G0, BK, Kraw, WfA, WfB, WbA, WbB, TT, PX, KX, GL, RS, RL,
    SS, x0r, g2r, kr, kxr, acr, grr, pxr, glr, rsr, azr, axr,
):
    s = lax.axis_index("section")
    t = lax.axis_index("tm")
    y = s // 2
    c = s % 2
    x = t // 8
    z = t % 8
    m = z // 4
    a = z % 4
    j = 4 * x + a + (x % 2) * (3 - 2 * a)
    q = t // 2
    e = t % 2
    first = c == 0
    second = c == 1
    drains = []

    def remote(src, dst, recv, dev, idx):
        return pltpu.make_async_remote_copy(
            src_ref=src, dst_ref=dst, send_sem=SS.at[idx], recv_sem=recv, device_id=dev, device_id_type=MESH
        )

    def send(src, dst, recv, dev, cond=None):
        idx = len(drains)
        make = lambda: remote(src, dst, recv, dev, idx)
        if cond is None:
            make().start()
        else:
            pl.when(cond)(lambda: make().start())
        drains.append((cond, make))

    def send_or_copy(src, dst, recv, dev, cond, own):
        send(src, dst, recv, dev, jnp.logical_and(cond, jnp.logical_not(own)))

        @pl.when(jnp.logical_and(cond, own))
        def _():
            pltpu.make_async_copy(src, dst, recv).start()

    def arrive(dst, recv):
        pltpu.make_async_remote_copy(
            src_ref=dst, dst_ref=dst, send_sem=SS.at[0], recv_sem=recv,
            device_id=(s - c + (1 - c), t), device_id_type=MESH,
        ).wait_recv()

    def arrive_if(cond, dst, recv):
        pl.when(cond)(lambda: arrive(dst, recv))

    both = jnp.logical_and

    for dj in (2, 1, 0, -1):
        for mm in range(2):
            there = q + dj
            ok = both(both(second, y == 0), both(there >= 0, there <= 15))
            to = tm_of(mm, there)
            send_or_copy(
                clips.at[mm], X0.at[(2 - dj) * 2 + e], x0r.at[2 - dj], (1, to), ok, to == t
            )
    send(k_ref, Kraw, kr, (s + 1, t), first)
    for dj in (0, -1, -2):
        for mm in range(2):
            there = q + dj
            ok = both(both(first, y == PLANES - 1), both(there >= 0, there <= 15))
            send(cot.at[mm], G2.at[-2 * dj + e], g2r.at[-dj], (2 * PLANES - 1, tm_of(mm, there)), ok)

    def fwd_weight(dst, src):
        for tap in range(27):
            dt, n = tap // 9, tap % 9
            dst[dt * 128 : (dt + 1) * 128, n * 128 : (n + 1) * 128] = src[tap]

    def bwd_weight(dst, src):
        for tap in range(27):
            dt, n = tap // 9, tap % 9
            dst[dt * 128 : (dt + 1) * 128, n * 128 : (n + 1) * 128] = src[26 - tap].astype(F32).T.astype(BF16)

    def frame_silu(ref, k):
        return silu(ref[k].astype(F32)).astype(BF16)

    def build_patches(ref, base):
        def one(k, carry):
            v = frame_silu(ref, base + k).astype(F32).reshape(16, 8, 128)
            for dw in range(3):
                vw = v if dw == 1 else shift_w(v, dw - 1)
                for dh in range(3):
                    vh = vw if dh == 1 else shift_h(vw, dh - 1)
                    TT[k, dh * 3 + dw] = vh.reshape(128, 128).T.astype(BF16)
            return carry

        lax.fori_loop(0, 4, one, 0)

    def block_a(lo, hi):
        out = conv([frame_silu(X0, k) for k in range(lo, hi + 2)], WfA)
        for k in range(lo, hi):
            X1[k] = (X0[k + 2].astype(F32) + out[k - lo]).astype(BF16)

    def block_b():
        out = conv([frame_silu(X1, k) for k in range(4)], WfB)
        for k in range(2):
            X2[k] = (X1[k + 2].astype(F32) + out[k]).astype(BF16)

    def back_a():
        out = conv([G2[k] for k in range(6)], WbB)
        for k in range(4):
            BK[k] = out[k]

    def out_home(src, dst, recv, core):
        for k in range(2):
            dev = (2 * y + core, 2 * j + k)
            if core == 0:
                send(src.at[k], dst.at[m], recv.at[m], dev, second)
            else:
                send_or_copy(src.at[k], dst.at[m], recv.at[m], dev, second, 2 * j + k == t)

    @pl.when(second)
    def _():
        zero2 = jnp.zeros((2, 128, 128), BF16)

        @pl.when(j < 2)
        def _():
            X0[0:2] = zero2

        @pl.when(j < 1)
        def _():
            X0[2:4] = zero2

        @pl.when(j > 14)
        def _():
            X0[6:8] = zero2
            G2[2:4] = zero2

        @pl.when(j > 13)
        def _():
            G2[4:6] = zero2

        fwd_weight(WfB, k_ref)
        arrive(Kraw, kr)
        fwd_weight(WfA, Kraw)

        @pl.when(y > 0)
        def _():
            bwd_weight(WbB, k_ref)
            bwd_weight(WbA, Kraw)

        @pl.when(y == PLANES - 1)
        def _():
            arrive(G2.at[0:2], g2r.at[0])
            arrive_if(j <= 14, G2.at[2:4], g2r.at[1])
            arrive_if(j <= 13, G2.at[4:6], g2r.at[2])
            back_a()

        arrive(X0.at[4:6], x0r.at[2])
        arrive_if(j >= 1, X0.at[2:4], x0r.at[1])

        @pl.when(y < PLANES - 1)
        def _():
            arrive_if(j >= 2, X0.at[0:2], x0r.at[0])
            block_a(0, 4)
            block_b()

        @pl.when(y == PLANES - 1)
        def _():
            arrive_if(j <= 14, X0.at[6:8], x0r.at[3])
            block_a(2, 6)

    for dj in (2, 1, 0, -1):
        there = j + dj
        ok = both(both(second, y < PLANES - 1), both(there >= 0, there <= 15))
        send(X2, X0.at[(2 - dj) * 2 : (2 - dj) * 2 + 2], x0r.at[2 - dj], (s + 2, tm_of(m, there)), ok)

    early = both(second, y < PLANES - 2)
    late = both(second, y >= PLANES - 2)

    @pl.when(both(second, y == 0))
    def _():
        bwd_weight(WbB, k_ref)
        bwd_weight(WbA, Kraw)

    @pl.when(both(second, y < PLANES - 1))
    def _():
        arrive_if(j <= 14, X0.at[6:8], x0r.at[3])
        block_a(4, 6)

    def swap_patches(cond):
        for d in range(4):
            other = (x + d) % 4
            src = TT.at[:, :, pl.ds(pl.multiple_of(32 * other, 32), 32), :]
            if d == 0:
                pl.when(cond)(lambda: pltpu.make_async_copy(src, PX.at[x], pxr.at[0]).start())
            else:
                send(src, PX.at[x], pxr.at[d], (s, other * 8 + z), cond)

    @pl.when(early)
    def _():
        build_patches(X1, 0)

    swap_patches(early)

    @pl.when(second)
    def _():
        @pl.when(y < PLANES - 1)
        def _():
            arrive(G2.at[0:2], g2r.at[0])
            arrive_if(j <= 14, G2.at[2:4], g2r.at[1])
            arrive_if(j <= 13, G2.at[4:6], g2r.at[2])
            back_a()

        for k in range(4):
            G1[k] = (G2[k].astype(F32) + BK[k] * silu_slope(X1[k + 2].astype(F32))).astype(BF16)
        out = conv([G1[k] for k in range(4)], WbA)
        for k in range(2):
            G0[k] = (G1[k].astype(F32) + out[k] * silu_slope(X0[k + 4].astype(F32))).astype(BF16)

    for dj in (-2, -1, 0):
        there = j + dj
        ok = both(both(second, y > 0), there >= 0)
        send(G0, G2.at[-2 * dj : -2 * dj + 2], g2r.at[-dj], (s - 2, tm_of(m, there)), ok)
    for d in range(4):
        other = (x + d) % 4
        send(G1.at[0:2], GL.at[x], glr.at[d], (s - 1, other * 8 + z), second)
    for d in range(1, 4):
        other = (x + d) % 4
        send(G2.at[0:2], GL.at[x], glr.at[d], (s, other * 8 + z), second)
    pl.when(second)(lambda: pltpu.make_async_copy(G2.at[0:2], GL.at[x], glr.at[0]).start())
    send(X0.at[2:6], KX, kxr, (s - 1, t), second)
    out_home(G0, grad, grr, 0)
    out_home(G1, grad, grr, 1)

    @pl.when(both(second, y == PLANES - 1))
    def _():
        arrive_if(j >= 2, X0.at[0:2], x0r.at[0])
        block_a(0, 2)
        block_b()

    out_home(X1.at[2:4], act, acr, 0)
    out_home(X2, act, acr, 1)

    @pl.when(first)
    def _():
        arrive(KX, kxr)
        build_patches(KX, 0)

    @pl.when(late)
    def _():
        build_patches(X1, 0)

    swap_patches(jnp.logical_or(first, late))

    for d in range(4):
        source = (x + 4 - d) % 4
        arrive(PX.at[source], pxr.at[d])
        arrive(GL.at[source], glr.at[d])
    for dt in range(3):
        total = None
        for p in range(4):
            left = jnp.concatenate(
                [PX[p, dt].reshape(288, 128), PX[p, dt + 1].reshape(288, 128)], axis=1
            )
            term = jnp.dot(left, GL[p].reshape(256, 128), preferred_element_type=F32)
            total = term if total is None else total + term
        RS[dt * 288 : (dt + 1) * 288, :] = total.astype(BF16)
    RS[864:896, :] = jnp.zeros((32, 128), BF16)

    def chunk(k):
        return pl.ds(pl.multiple_of(k * ROWS, 16), ROWS)

    for d in range(1, 8):
        other = (z + d) % 8
        send(RS.at[chunk(other)], RL.at[z], rsr.at[d], (s, x * 8 + other))
    total = RS[chunk(z), :].astype(F32)
    for d in range(1, 8):
        source = (z + 8 - d) % 8
        arrive(RL.at[source], rsr.at[d])
        total = total + RL[source].astype(F32)
    mine = kg.at[x, chunk(z)]
    mine[...] = total.astype(BF16)
    for d in range(1, 8):
        other = (z + d) % 8
        send(mine, mine, azr.at[d], (s, x * 8 + other))
    for d in range(1, 8):
        source = (z + 8 - d) % 8
        arrive(kg.at[x, chunk(source)], azr.at[d])
    for d in range(1, 4):
        other = (x + d) % 4
        send(kg.at[x], kg.at[x], axr.at[d], (s, other * 8 + z))
    for d in range(1, 4):
        source = (x + 4 - d) % 4
        arrive(kg.at[source], axr.at[d])
    for mm in range(2):
        arrive(act.at[mm], acr.at[mm])
        arrive(grad.at[mm], grr.at[mm])
    for cond, make in drains:
        if cond is None:
            make().wait_send()
        else:
            pl.when(cond)(lambda make=make: make().wait_send())


def body(clips, kernels, cotangent):
    micro, frames, height, width, chan = clips.shape
    vmem = pl.BlockSpec(memory_space=pltpu.VMEM)
    frame = lambda n: pltpu.VMEM((n, 128, 128), BF16)
    weight = pltpu.VMEM((384, 1152), BF16)
    dma = pltpu.SemaphoreType.DMA
    act, grad, kg = pl.pallas_call(
        kernel,
        out_shape=(
            jax.ShapeDtypeStruct((2, 128, 128), BF16),
            jax.ShapeDtypeStruct((2, 128, 128), BF16),
            jax.ShapeDtypeStruct((4, 8 * ROWS, 128), BF16),
        ),
        in_specs=[vmem] * 3,
        out_specs=(vmem,) * 3,
        scratch_shapes=[
            frame(8), frame(6), frame(2), frame(6), frame(4), frame(2),
            pltpu.VMEM((4, 128, 128), F32),
            frame(27), weight, weight, weight, weight,
            pltpu.VMEM((4, 9, 128, 128), BF16),
            pltpu.VMEM((4, 4, 9, 32, 128), BF16),
            frame(4),
            pltpu.VMEM((4, 2, 128, 128), BF16),
            pltpu.VMEM((8 * ROWS, 128), BF16),
            pltpu.VMEM((8, ROWS, 128), BF16),
            dma((80,)), dma((4,)), dma((3,)), dma, dma, dma((2,)), dma((2,)),
            dma((4,)), dma((4,)), dma((8,)), dma((8,)), dma((4,)),
        ],
        compiler_params=pltpu.CompilerParams(has_side_effects=True, vmem_limit_bytes=48 << 20),
        name="blocks",
    )(
        clips.reshape(2, 128, 128),
        kernels.reshape(27, 128, 128),
        cotangent.reshape(2, 128, 128),
    )
    total = micro * frames * lax.axis_size("tm") * height * width
    norm = 1.0 / jnp.sqrt(jnp.float32(total))
    parts = kg[:, :864].reshape(4, 27, 32, 128).transpose(1, 0, 2, 3).astype(F32) * norm
    return (
        act.reshape(1, micro, 1, height, width, chan),
        grad.reshape(1, micro, 1, height, width, chan),
        parts.reshape(1, 3, 3, 3, chan, chan),
    )


def solution(mesh):
    placed = (
        P(None, "tm", None, None, None),
        P("section", None, None, None, None, None),
        P(None, "tm", None, None, None),
    )
    return jax.shard_map(
        body,
        mesh=mesh,
        in_specs=placed,
        out_specs=(
            P("section", None, "tm", None, None, None),
            P("section", None, "tm", None, None, None),
            P("section", None, None, None, None, None),
        ),
        check_vma=False,
    )
```

time: 1150 us -> 149 us (0.13)
  the two profiles are of different devices: /device:TPU:1 before, /device:TPU:4 now
where the time goes in v1:
time: 149 us
  Pallas kernels  143 us (96%)
  local copies, waits for them, and re-layouts  5.48 us (4%)
    pallas_call x1, Pallas kernels, body(): pl.pallas_call(kernel, out_shape=(jax.ShapeDtypeStruct((2, 128, 128), BF1...  143 us
    unnamed x8, local copies, waits for them, and re-layouts  4.1 us

profile of v1, /device:TPU:4, one launch (start us, length us, event | category | flops | bytes accessed | tf_op | source)
XLA Modules:
  0.0 148.8 jit_solution(15668763954761343372)
XLA Ops:
  0.6 0.0 copy-start
  0.6 1.2 copy-done
  1.8 0.0 copy-start.1
  1.8 0.8 copy-done.1
  2.6 0.0 copy-start.2
  2.6 0.8 copy-done.2
  3.5 142.5 %blocks.1 = (bf16[2,128,128]{2,1,0:T(8,128)(2,1)S(1)}, bf16[2,128,128]{2,1,0:T(8,128)(2,1)S(1)}, bf16[4,896,128]{2,1,0:T(8,128)(2,1)S(1)}) custom-call(bf16[2,128,128]{2,1,0:T(8,128)(2,1)S(1)} %bitcast.14, bf16[27,128,128]{2,1,0:T(8,128)(2,1)S(1)} %bitcast.13, bf16[2,128,128]{2,1,0:T(8,128)(2,1)S(1)} %bitcast.15), custom_call_target="tpu_custom_call" | custom-call | tf_op jit(solution)/shard_map/blocks/pallas_call | solution.py:365
  146.0 0.1 convert_multiply_fusion
  146.2 1.4 copy.6
  147.5 0.6 copy.11
  148.2 0.6 copy.12
Async XLA Ops:
  0.6 1.2 copy-start
  1.8 0.8 copy-start.1
  2.6 0.8 copy-start.2

commit v2 on v1

v2 whole, which is shorter than its diff:
```python
import functools

import jax
import jax.numpy as jnp
from jax import lax
from jax.experimental import pallas as pl
from jax.experimental.pallas import tpu as pltpu
from jax.sharding import PartitionSpec as P

MESH = pl.DeviceIdType.MESH
PLANES = 8
ROWS = 112
BF16 = jnp.bfloat16
F32 = jnp.float32


def logistic(v):
    return 0.5 + 0.5 * jnp.tanh(0.5 * v)


def silu(v):
    return v * logistic(v)


def silu_slope(v):
    sig = logistic(v)
    return sig * (1.0 + v * (1.0 - sig))


def shift_w(a, d):
    r = pltpu.roll(a, (-d) % 8, 1)
    w = lax.broadcasted_iota(jnp.int32, a.shape, 1)
    return jnp.where(w < 7, r, 0.0) if d == 1 else jnp.where(w > 0, r, 0.0)


def shift_h(a, d):
    z = jnp.zeros((1,) + a.shape[1:], a.dtype)
    return jnp.concatenate([a[1:], z], axis=0) if d == 1 else jnp.concatenate([z, a[:-1]], axis=0)


def conv(frames, weight):
    count = len(frames) - 2
    rows = [jnp.concatenate(frames[f : f + 3], axis=1) for f in range(count)]
    left = jnp.concatenate(rows, axis=0) if count > 1 else rows[0]
    full = jnp.dot(left, weight[...], preferred_element_type=F32)
    outs = []
    for f in range(count):
        part = full[f * 128 : (f + 1) * 128]
        cols = []
        for dw in range(3):
            g = [part[:, (dh * 3 + dw) * 128 : (dh * 3 + dw + 1) * 128].reshape(16, 8, 128) for dh in range(3)]
            cols.append(g[1] + shift_h(g[0], -1) + shift_h(g[2], 1))
        acc = cols[1] + shift_w(cols[0], -1) + shift_w(cols[2], 1)
        outs.append(acc.reshape(128, 128))
    return outs


def tm_of(m, j):
    b, xx = j // 8, j % 8 // 2
    return (xx + b * (3 - 2 * xx)) * 8 + 4 * m + 2 * b + j % 2


def kernel(
    clips, k_hbm, cot, act, grad, kg,
    X0, X1, X2, G2, G1, G0, BK, S1, S0, WfA, WfB, WbA, WbB, KX, AG,
    TT, PX, GL, RS, RL, TT2, PX2, GL2, RS2, RL2,
    SS, ownr, x0r, g2r, kr, kxr, acr, grr, pxr, glr, rsr, px2r, gl2r, rs2r, kgr, azr, axr, az2r, ax2r,
):
    s = lax.axis_index("section")
    t = lax.axis_index("tm")
    y = s // 2
    c = s % 2
    x = t // 8
    z = t % 8
    m = z // 4
    b = z % 4 // 2
    j = 8 * b + 2 * (x + b * (3 - 2 * x)) + z % 2
    q = t // 2
    e = t % 2
    first = c == 0
    second = c == 1
    drains = []
    both = jnp.logical_and

    def remote(src, dst, recv, dev, idx):
        return pltpu.make_async_remote_copy(
            src_ref=src, dst_ref=dst, send_sem=SS.at[idx], recv_sem=recv, device_id=dev, device_id_type=MESH
        )

    def send(src, dst, recv, dev, cond=None):
        idx = len(drains)
        make = lambda: remote(src, dst, recv, dev, idx)
        if cond is None:
            make().start()
        else:
            pl.when(cond)(lambda: make().start())
        drains.append((cond, make))

    def send_or_copy(src, dst, recv, dev, cond, own):
        send(src, dst, recv, dev, jnp.logical_and(cond, jnp.logical_not(own)))

        @pl.when(jnp.logical_and(cond, own))
        def _():
            pltpu.make_async_copy(src, dst, recv).start()

    def arrive(dst, recv):
        pltpu.make_async_remote_copy(
            src_ref=dst, dst_ref=dst, send_sem=SS.at[0], recv_sem=recv,
            device_id=(s - c + (1 - c), t), device_id_type=MESH,
        ).wait_recv()

    def arrive_if(cond, dst, recv):
        pl.when(cond)(lambda: arrive(dst, recv))

    def tap_block(ref, tap):
        dt, n = tap // 9, tap % 9
        return ref.at[dt * 128 : (dt + 1) * 128, n * 128 : (n + 1) * 128]

    @pl.when(second)
    def _():
        for tap in range(27):
            pltpu.make_async_copy(k_hbm.at[tap], tap_block(WfB, tap), ownr).start()

    entry = pltpu.get_barrier_semaphore()
    expected = []

    def greet(cond, dev):
        pl.when(cond)(lambda: pl.semaphore_signal(entry, inc=1, device_id=dev, device_id_type=MESH))

    def expect(cond):
        expected.append(cond.astype(jnp.int32))

    inside = lambda v, top: both(v >= 0, v <= top)
    for k in range(-4, 4):
        at = 2 * j + k
        greet(both(both(second, y == 0), both(inside(at, 31), at != t)), (1, at))
    for dj in (2, 1, 0, -1):
        for mm in range(2):
            ok = both(both(second, y == 0), inside(q + dj, 15))
            expect(both(ok, tm_of(mm, q + dj) != t))
    for dj in (2, 1, 0, -1):
        greet(both(both(second, y > 0), inside(j - dj, 15)), (s - 2, tm_of(m, j - dj)))
        expect(both(both(second, y < PLANES - 1), inside(j + dj, 15)))
    for dj in (-2, -1, 0):
        greet(both(both(second, y < PLANES - 1), inside(j - dj, 15)), (s + 2, tm_of(m, j - dj)))
        expect(both(both(second, y > 0), inside(j + dj, 15)))
    for k in range(6):
        at = 2 * j + k
        greet(both(both(second, y == PLANES - 1), at <= 31), (2 * PLANES - 2, at))
    for dj in (0, -1, -2):
        for mm in range(2):
            expect(both(both(first, y == PLANES - 1), inside(q + dj, 15)))
    always = s >= 0
    for d in range(4):
        greet(first, (s + 1, (x + d) % 4 * 8 + z))
        expect(second)
    greet(second, (s - 1, t))
    expect(first)
    greet(both(first, y > 0), (s - 1, t))
    expect(both(second, y < PLANES - 1))
    greet(both(second, y < PLANES - 1), (s + 1, t))
    expect(both(first, y > 0))
    for d in range(1, 4):
        greet(always, (s, (x + d) % 4 * 8 + z))
        expect(always)
    for d in range(1, 8):
        greet(always, (s, x * 8 + (z + d) % 8))
        expect(always)
    for mm in range(2):
        at = tm_of(mm, q)
        greet(jnp.logical_or(first, at != t), (2 * y + 1, at))
    for k in range(2):
        expect(second)
        expect(both(second, 2 * j + k != t))
    pl.semaphore_wait(entry, sum(expected))

    for dj in (2, 1, 0, -1):
        for mm in range(2):
            there = q + dj
            ok = both(both(second, y == 0), both(there >= 0, there <= 15))
            to = tm_of(mm, there)
            send_or_copy(
                clips.at[mm], X0.at[(2 - dj) * 2 + e], x0r.at[2 - dj], (1, to), ok, to == t
            )
    idx = len(drains)
    all_taps = lambda: remote(k_hbm, k_hbm, kr, (s + 1, t), idx)
    drains.append((first, all_taps))

    @pl.when(first)
    def _():
        for tap in range(27):
            remote(k_hbm.at[tap], tap_block(WfA, tap), kr, (s + 1, t), idx).start()

    for dj in (0, -1, -2):
        for mm in range(2):
            there = q + dj
            ok = both(both(first, y == PLANES - 1), both(there >= 0, there <= 15))
            send(cot.at[mm], G2.at[-2 * dj + e], g2r.at[-dj], (2 * PLANES - 1, tm_of(mm, there)), ok)

    def bwd_weight(dst, src):
        for tap in range(27):
            tap_block(dst, tap)[...] = tap_block(src, 26 - tap)[...].astype(F32).T.astype(BF16)

    def frame_silu(ref, k):
        return silu(ref[k].astype(F32)).astype(BF16)

    def build_patches(ref, TT):
        def one(k, carry):
            v = frame_silu(ref, k).astype(F32).reshape(16, 8, 128)
            for dw in range(3):
                vw = v if dw == 1 else shift_w(v, dw - 1)
                for dh in range(3):
                    vh = vw if dh == 1 else shift_h(vw, dh - 1)
                    TT[k, dh * 3 + dw] = vh.reshape(128, 128).T.astype(BF16)
            return carry

        lax.fori_loop(0, 4, one, 0)

    def block_a(lo, hi):
        out = conv([frame_silu(X0, k) for k in range(lo, hi + 2)], WfA)
        for k in range(lo, hi):
            X1[k] = (X0[k + 2].astype(F32) + out[k - lo]).astype(BF16)

    def block_b():
        out = conv([frame_silu(X1, k) for k in range(4)], WfB)
        for k in range(2):
            X2[k] = (X1[k + 2].astype(F32) + out[k]).astype(BF16)

    def back_a():
        out = conv([G2[k] for k in range(6)], WbB)
        for k in range(4):
            BK[k] = out[k]

    def out_home(src, dst, recv, core, cond):
        for k in range(2):
            dev = (2 * y + core, 2 * j + k)
            if core == 0:
                send(src.at[k], dst.at[m], recv.at[m], dev, cond)
            else:
                send_or_copy(src.at[k], dst.at[m], recv.at[m], dev, cond, 2 * j + k == t)

    @pl.when(second)
    def _():
        zero2 = jnp.zeros((2, 128, 128), BF16)

        @pl.when(j < 2)
        def _():
            X0[0:2] = zero2

        @pl.when(j < 1)
        def _():
            X0[2:4] = zero2

        @pl.when(j > 14)
        def _():
            X0[6:8] = zero2
            G2[2:4] = zero2

        @pl.when(j > 13)
        def _():
            G2[4:6] = zero2

        pltpu.make_async_copy(WfB, WfB, ownr).wait()
        arrive(WfA, kr)

        @pl.when(y > 0)
        def _():
            bwd_weight(WbB, WfB)
            bwd_weight(WbA, WfA)

        @pl.when(y == PLANES - 1)
        def _():
            arrive(G2.at[0:2], g2r.at[0])
            arrive_if(j <= 14, G2.at[2:4], g2r.at[1])
            arrive_if(j <= 13, G2.at[4:6], g2r.at[2])
            back_a()

        arrive(X0.at[4:6], x0r.at[2])
        arrive_if(j >= 1, X0.at[2:4], x0r.at[1])

        @pl.when(y < PLANES - 1)
        def _():
            arrive_if(j >= 2, X0.at[0:2], x0r.at[0])
            block_a(0, 4)
            block_b()

        @pl.when(y == PLANES - 1)
        def _():
            arrive_if(j <= 14, X0.at[6:8], x0r.at[3])
            block_a(2, 6)

    forward = both(second, y < PLANES - 1)
    fast = []

    def flush():
        while fast:
            cond, make = fast.pop()
            pl.when(cond)(lambda make=make: make().wait_send())

    def send_fast(src, dst, recv, dev, cond):
        send(src, dst, recv, dev, cond)
        fast.append(drains[-1])
        drains[-1] = None

    for dj in (2, 1, 0, -1):
        there = j + dj
        ok = both(forward, inside(there, 15))
        send_fast(X2, X0.at[(2 - dj) * 2 : (2 - dj) * 2 + 2], x0r.at[2 - dj], (s + 2, tm_of(m, there)), ok)

    top = both(second, y == PLANES - 1)

    @pl.when(both(second, y == 0))
    def _():
        bwd_weight(WbB, WfB)
        bwd_weight(WbA, WfA)

    @pl.when(both(second, y < PLANES - 1))
    def _():
        arrive_if(j <= 14, X0.at[6:8], x0r.at[3])
        block_a(4, 6)

    flush()
    send(X1.at[0:4], KX, kxr, (s + 1, t), forward)

    def swap_patches(cond, TT, PX, pxr):
        for d in range(4):
            other = (x + d) % 4
            src = TT.at[:, :, pl.ds(pl.multiple_of(32 * other, 32), 32), :]
            if d == 0:
                pl.when(cond)(lambda: pltpu.make_async_copy(src, PX.at[x], pxr.at[0]).start())
            else:
                send(src, PX.at[x], pxr.at[d], (s, other * 8 + z), cond)

    @pl.when(forward)
    def _():
        build_patches(X0.at[2:6], TT)

    swap_patches(forward, TT, PX, pxr)
    out_home(X1.at[2:4], act, acr, 0, forward)
    out_home(X2, act, acr, 1, forward)

    @pl.when(second)
    def _():
        for k in range(4):
            S1[k] = silu_slope(X1[k + 2].astype(F32))
        for k in range(2):
            S0[k] = silu_slope(X0[k + 4].astype(F32))

        @pl.when(y < PLANES - 1)
        def _():
            arrive(G2.at[0:2], g2r.at[0])
            arrive_if(j <= 14, G2.at[2:4], g2r.at[1])
            arrive_if(j <= 13, G2.at[4:6], g2r.at[2])
            back_a()

        for k in range(4):
            G1[k] = (G2[k].astype(F32) + BK[k] * S1[k]).astype(BF16)

    def gather(src, GL, glr, cond):
        for d in (2, 1, 3):
            other = (x + d) % 4
            send(src, GL.at[x], glr.at[d], (s, other * 8 + z), cond)
        pl.when(cond)(lambda: pltpu.make_async_copy(src, GL.at[x], glr.at[0]).start())

    gather(G1.at[0:2], GL, glr, both(second, y == 0))

    @pl.when(second)
    def _():
        out = conv([G1[k] for k in range(4)], WbA)
        for k in range(2):
            G0[k] = (G1[k].astype(F32) + out[k] * S0[k]).astype(BF16)

    for dj in (-2, -1, 0):
        there = j + dj
        ok = both(both(second, y > 0), there >= 0)
        send_fast(G0, G2.at[-2 * dj : -2 * dj + 2], g2r.at[-dj], (s - 2, tm_of(m, there)), ok)
    flush()
    behind = both(second, y > 0)
    for d in (2, 1, 3, 0):
        other = (x + d) % 4
        send(G0, GL.at[x], glr.at[d], (s - 1, other * 8 + z), behind)
    gather(G1.at[0:2], GL, glr, behind)
    gather(G2.at[0:2], GL2, gl2r, top)
    out_home(G0, grad, grr, 0, second)
    out_home(G1, grad, grr, 1, second)

    @pl.when(top)
    def _():
        arrive_if(j >= 2, X0.at[0:2], x0r.at[0])
        block_a(0, 2)
        block_b()
        build_patches(X0.at[2:6], TT)
        build_patches(X1, TT2)

    out_home(X1.at[2:4], act, acr, 0, top)
    out_home(X2, act, acr, 1, top)
    swap_patches(top, TT2, PX2, px2r)

    lower = both(first, y > 0)

    @pl.when(lower)
    def _():
        arrive(KX, kxr)
        build_patches(KX, TT)

    swap_patches(jnp.logical_or(lower, top), TT, PX, pxr)

    def chunk(k):
        return pl.ds(pl.multiple_of(k * ROWS, 16), ROWS)

    def reduce_terms(cond, PX, GL, RS, RL, pxr, glr, rsr, out):
        @pl.when(cond)
        def _():
            for d in range(4):
                source = (x + 4 - d) % 4
                arrive(PX.at[source], pxr.at[d])
                arrive(GL.at[source], glr.at[d])
            for dt in range(3):
                total = None
                for p in range(4):
                    left = jnp.concatenate(
                        [PX[p, dt].reshape(288, 128), PX[p, dt + 1].reshape(288, 128)], axis=1
                    )
                    term = jnp.dot(left, GL[p].reshape(256, 128), preferred_element_type=F32)
                    total = term if total is None else total + term
                RS[dt * 288 : (dt + 1) * 288, :] = total.astype(BF16)
            RS[864:896, :] = jnp.zeros((32, 128), BF16)

        for d in (4, 3, 5, 2, 6, 1, 7):
            other = (z + d) % 8
            send(RS.at[chunk(other)], RL.at[z], rsr.at[d], (s, x * 8 + other), cond)

        @pl.when(cond)
        def _():
            total = RS[chunk(z), :].astype(F32)
            for d in range(1, 8):
                source = (z + 8 - d) % 8
                arrive(RL.at[source], rsr.at[d])
                total = total + RL[source].astype(F32)
            out[...] = total.astype(BF16)

    right, left, far = (x + 1) % 4, (x + 3) % 4, (x + 2) % 4
    order = (0, 1, 7, 2, 6, 3, 5, 4)

    def gather_sum(cond, buf, azr, axr, deliver):
        piece = lambda ref, row, d: ref.at[row, chunk((z + 8 - d) % 8)]

        def pass_on(row, d, recv, dev):
            send(piece(buf, row, d), piece(buf, row, d), recv, dev, cond)

        def hand_over(row, d):
            if deliver:
                send(piece(buf, row, d), piece(kg, row, d), kgr, (s - 1, t), cond)

        for d in (4, 3, 5, 2, 6, 1, 7):
            pass_on(x, 0, azr.at[d], (s, x * 8 + (z + d) % 8))
        for d in order:
            if d:
                arrive_if(cond, piece(buf, x, d), azr.at[d])
            pass_on(x, d, axr.at[0, d], (s, right * 8 + z))
            pass_on(x, d, axr.at[1, d], (s, left * 8 + z))
        for at, d in enumerate(order):
            arrive_if(cond, piece(buf, left, d), axr.at[0, d])
            arrive_if(cond, piece(buf, right, d), axr.at[1, d])
            if at % 2:
                pass_on(left, d, axr.at[2, d], (s, right * 8 + z))
            else:
                pass_on(right, d, axr.at[2, d], (s, left * 8 + z))
            hand_over(x, d)
        for d in order:
            hand_over(left, d)
            hand_over(right, d)
        for d in order:
            arrive_if(cond, piece(buf, far, d), axr.at[2, d])
            hand_over(far, d)

    working = s > 0
    reduce_terms(working, PX, GL, RS, RL, pxr, glr, rsr, AG.at[x, chunk(z)])
    gather_sum(working, AG, azr, axr, True)
    reduce_terms(top, PX2, GL2, RS2, RL2, px2r, gl2r, rs2r, kg.at[x, chunk(z)])
    gather_sum(top, kg, az2r, ax2r, False)
    arrive_if(s < 2 * PLANES - 1, kg, kgr)
    for mm in range(2):
        arrive(act.at[mm], acr.at[mm])
        arrive(grad.at[mm], grr.at[mm])
    for cond, make in filter(None, drains):
        if cond is None:
            make().wait_send()
        else:
            pl.when(cond)(lambda make=make: make().wait_send())


def body(clips, kernels, cotangent):
    micro, frames, height, width, chan = clips.shape
    vmem = pl.BlockSpec(memory_space=pltpu.VMEM)
    frame = lambda n: pltpu.VMEM((n, 128, 128), BF16)
    weight = pltpu.VMEM((384, 1152), BF16)
    dma = pltpu.SemaphoreType.DMA
    terms = (
        pltpu.VMEM((4, 9, 128, 128), BF16),
        pltpu.VMEM((4, 4, 9, 32, 128), BF16),
        pltpu.VMEM((4, 2, 128, 128), BF16),
        pltpu.VMEM((8 * ROWS, 128), BF16),
        pltpu.VMEM((8, ROWS, 128), BF16),
    )
    act, grad, kg = pl.pallas_call(
        kernel,
        out_shape=(
            jax.ShapeDtypeStruct((2, 128, 128), BF16),
            jax.ShapeDtypeStruct((2, 128, 128), BF16),
            jax.ShapeDtypeStruct((4, 8 * ROWS, 128), BF16),
        ),
        in_specs=[pl.BlockSpec(memory_space=pl.ANY)] * 3,
        out_specs=(vmem,) * 3,
        scratch_shapes=[
            frame(8), frame(6), frame(2), frame(6), frame(4), frame(2),
            pltpu.VMEM((4, 128, 128), F32),
            pltpu.VMEM((4, 128, 128), F32),
            pltpu.VMEM((2, 128, 128), F32),
            weight, weight, weight, weight, frame(4), pltpu.VMEM((4, 8 * ROWS, 128), BF16),
            *terms, *terms,
            dma((210,)), dma, dma((4,)), dma((3,)), dma, dma, dma((2,)), dma((2,)),
            dma((4,)), dma((4,)), dma((8,)), dma((4,)), dma((4,)), dma((8,)),
            dma, dma((8,)), dma((3, 8)), dma((8,)), dma((3, 8)),
        ],
        compiler_params=pltpu.CompilerParams(
            collective_id=0, has_side_effects=True, vmem_limit_bytes=48 << 20,
        ),
        name="blocks",
    )(
        clips.reshape(2, 128, 128),
        kernels.reshape(27, 128, 128),
        cotangent.reshape(2, 128, 128),
    )
    total = micro * frames * lax.axis_size("tm") * height * width
    norm = 1.0 / jnp.sqrt(jnp.float32(total))
    parts = kg[:, :864].reshape(4, 27, 32, 128).transpose(1, 0, 2, 3).astype(F32) * norm
    return (
        act.reshape(1, micro, 1, height, width, chan),
        grad.reshape(1, micro, 1, height, width, chan),
        parts.reshape(1, 3, 3, 3, chan, chan),
    )


def solution(mesh):
    placed = (
        P(None, "tm", None, None, None),
        P("section", None, None, None, None, None),
        P(None, "tm", None, None, None),
    )
    return jax.shard_map(
        body,
        mesh=mesh,
        in_specs=placed,
        out_specs=(
            P("section", None, "tm", None, None, None),
            P("section", None, "tm", None, None, None),
            P("section", None, None, None, None, None),
        ),
        check_vma=False,
    )
```

time: 149 us -> 141 us (0.946)
  the two profiles are of different devices: /device:TPU:4 before, /device:TPU:1 now
where the time goes in v2:
time: 141 us
  Pallas kernels  134 us (95%)
  local copies, waits for them, and re-layouts  5.48 us (4%)
    pallas_call x1, Pallas kernels, body(): pl.pallas_call(kernel, out_shape=(jax.ShapeDtypeStruct((2, 128, 128), BF1...  134 us
    unnamed x8, local copies, waits for them, and re-layouts  4.1 us

profile of v2, /device:TPU:1, one launch (start us, length us, event | category | flops | bytes accessed | tf_op | source)
XLA Modules:
  0.0 140.7 jit_solution(14092331451995267594)
XLA Ops:
  0.6 0.0 copy-start
  0.6 1.2 copy-done
  1.8 0.0 copy-start.1
  1.8 0.8 copy-done.1
  2.6 0.0 copy-start.2
  2.6 0.8 copy-done.2
  3.5 134.4 %blocks.1 = (bf16[2,128,128]{2,1,0:T(8,128)(2,1)S(1)}, bf16[2,128,128]{2,1,0:T(8,128)(2,1)S(1)}, bf16[4,896,128]{2,1,0:T(8,128)(2,1)S(1)}) custom-call(bf16[2,128,128]{2,1,0:T(8,128)(2,1)S(1)} %bitcast.14, bf16[27,128,128]{2,1,0:T(8,128)(2,1)S(1)} %bitcast.13, bf16[2,128,128]{2,1,0:T(8,128)(2,1)S(1)} %bitcast.15), custom_call_target="tpu_custom_call" | custom-call | tf_op jit(solution)/shard_map/blocks/pallas_call | solution.py:506
  137.9 0.1 convert_multiply_fusion
  138.1 1.4 copy.6
  139.5 0.6 copy.11
  140.1 0.6 copy.12
Async XLA Ops:
  0.6 1.2 copy-start
  1.8 0.8 copy-start.1
  2.6 0.8 copy-start.2

commit v3 on v2

--- a/solution.py
+++ b/solution.py
@@ -62,9 +62,9 @@
 
 def kernel(
     clips, k_hbm, cot, act, grad, kg,
-    X0, X1, X2, G2, G1, G0, BK, S1, S0, WfA, WfB, WbA, WbB, KX, AG,
+    X0, X1, X2, G2, G1, G0, BK, S1, S0, SX, WfA, WfB, WbA, WbB, KX, AG,
     TT, PX, GL, RS, RL, TT2, PX2, GL2, RS2, RL2,
-    SS, ownr, x0r, g2r, kr, kxr, acr, grr, pxr, glr, rsr, px2r, gl2r, rs2r, kgr, azr, axr, az2r, ax2r,
+    SS, ownr, x0r, g2r, kr, kxr, acr, grr, pxr, glr, rsr, px2r, gl2r, rs2r, kgr, chr, azr, axr, az2r, ax2r,
 ):
     s = lax.axis_index("section")
     t = lax.axis_index("tm")
@@ -115,11 +115,6 @@
     def tap_block(ref, tap):
         dt, n = tap // 9, tap % 9
         return ref.at[dt * 128 : (dt + 1) * 128, n * 128 : (n + 1) * 128]
-
-    @pl.when(second)
-    def _():
-        for tap in range(27):
-            pltpu.make_async_copy(k_hbm.at[tap], tap_block(WfB, tap), ownr).start()
 
     entry = pltpu.get_barrier_semaphore()
     expected = []
@@ -172,6 +167,11 @@
     for k in range(2):
         expect(second)
         expect(both(second, 2 * j + k != t))
+    @pl.when(second)
+    def _():
+        for tap in range(27):
+            pltpu.make_async_copy(k_hbm.at[tap], tap_block(WfB, tap), ownr).start()
+
     pl.semaphore_wait(entry, sum(expected))
 
     for dj in (2, 1, 0, -1):
@@ -216,8 +216,12 @@
 
         lax.fori_loop(0, 4, one, 0)
 
+    def take(k):
+        for at in (k, k + 1):
+            SX[at] = frame_silu(X0, at)
+
     def block_a(lo, hi):
-        out = conv([frame_silu(X0, k) for k in range(lo, hi + 2)], WfA)
+        out = conv([SX[k] for k in range(lo, hi + 2)], WfA)
         for k in range(lo, hi):
             X1[k] = (X0[k + 2].astype(F32) + out[k - lo]).astype(BF16)
 
@@ -226,10 +230,11 @@
         for k in range(2):
             X2[k] = (X1[k + 2].astype(F32) + out[k]).astype(BF16)
 
-    def back_a():
-        out = conv([G2[k] for k in range(6)], WbB)
-        for k in range(4):
-            BK[k] = out[k]
+    def back_a(k):
+        return conv([G2[at] for at in range(k, k + 4)], WbB)
+
+    def grad_a(k, back):
+        G1[k] = (G2[k].astype(F32) + back * S1[k]).astype(BF16)
 
     def out_home(src, dst, recv, core, cond):
         for k in range(2):
@@ -273,21 +278,31 @@
             arrive(G2.at[0:2], g2r.at[0])
             arrive_if(j <= 14, G2.at[2:4], g2r.at[1])
             arrive_if(j <= 13, G2.at[4:6], g2r.at[2])
-            back_a()
+            BK[0], BK[1] = back_a(0)
+            BK[2], BK[3] = back_a(2)
+
+        arrive_if(j >= 1, X0.at[2:4], x0r.at[1])
+        take(2)
+
+        @pl.when(y < PLANES - 1)
+        def _():
+            arrive_if(j >= 2, X0.at[0:2], x0r.at[0])
+            take(0)
+            block_a(0, 2)
 
         arrive(X0.at[4:6], x0r.at[2])
-        arrive_if(j >= 1, X0.at[2:4], x0r.at[1])
+        take(4)
+        block_a(2, 4)
 
         @pl.when(y < PLANES - 1)
         def _():
-            arrive_if(j >= 2, X0.at[0:2], x0r.at[0])
-            block_a(0, 4)
             block_b()
 
         @pl.when(y == PLANES - 1)
         def _():
             arrive_if(j <= 14, X0.at[6:8], x0r.at[3])
-            block_a(2, 6)
+            take(6)
+            block_a(4, 6)
 
     forward = both(second, y < PLANES - 1)
     fast = []
@@ -302,9 +317,15 @@
         fast.append(drains[-1])
         drains[-1] = None
 
-    for dj in (2, 1, 0, -1):
+    odd = j % 2 == 1
+    even = j % 2 == 0
+    for dj, when in ((1, odd), (2, None), (1, even), (0, None), (-1, y == PLANES - 2), (-1, y < PLANES - 2)):
         there = j + dj
         ok = both(forward, inside(there, 15))
+        if when is not None:
+            ok = both(ok, when)
+        if len(fast) == 5:
+            flush()
         send_fast(X2, X0.at[(2 - dj) * 2 : (2 - dj) * 2 + 2], x0r.at[2 - dj], (s + 2, tm_of(m, there)), ok)
 
     top = both(second, y == PLANES - 1)
@@ -317,6 +338,7 @@
     @pl.when(both(second, y < PLANES - 1))
     def _():
         arrive_if(j <= 14, X0.at[6:8], x0r.at[3])
+        take(6)
         block_a(4, 6)
 
     flush()
@@ -348,13 +370,18 @@
 
         @pl.when(y < PLANES - 1)
         def _():
-            arrive(G2.at[0:2], g2r.at[0])
             arrive_if(j <= 14, G2.at[2:4], g2r.at[1])
             arrive_if(j <= 13, G2.at[4:6], g2r.at[2])
-            back_a()
-
-        for k in range(4):
-            G1[k] = (G2[k].astype(F32) + BK[k] * S1[k]).astype(BF16)
+            for k, back in zip((2, 3), back_a(2)):
+                grad_a(k, back)
+            arrive(G2.at[0:2], g2r.at[0])
+            for k, back in zip((0, 1), back_a(0)):
+                grad_a(k, back)
+
+        @pl.when(y == PLANES - 1)
+        def _():
+            for k in range(4):
+                grad_a(k, BK[k])
 
     def gather(src, GL, glr, cond):
         for d in (2, 1, 3):
@@ -370,9 +397,11 @@
         for k in range(2):
             G0[k] = (G1[k].astype(F32) + out[k] * S0[k]).astype(BF16)
 
-    for dj in (-2, -1, 0):
+    for dj, when in ((-1, even), (-2, None), (-1, odd), (0, None)):
         there = j + dj
         ok = both(both(second, y > 0), there >= 0)
+        if when is not None:
+            ok = both(ok, when)
         send_fast(G0, G2.at[-2 * dj : -2 * dj + 2], g2r.at[-dj], (s - 2, tm_of(m, there)), ok)
     flush()
     behind = both(second, y > 0)
@@ -387,6 +416,7 @@
     @pl.when(top)
     def _():
         arrive_if(j >= 2, X0.at[0:2], x0r.at[0])
+        take(0)
         block_a(0, 2)
         block_b()
         build_patches(X0.at[2:6], TT)
@@ -442,44 +472,57 @@
     right, left, far = (x + 1) % 4, (x + 3) % 4, (x + 2) % 4
     order = (0, 1, 7, 2, 6, 3, 5, 4)
 
-    def gather_sum(cond, buf, azr, axr, deliver):
-        piece = lambda ref, row, d: ref.at[row, chunk((z + 8 - d) % 8)]
-
-        def pass_on(row, d, recv, dev):
-            send(piece(buf, row, d), piece(buf, row, d), recv, dev, cond)
-
-        def hand_over(row, d):
-            if deliver:
-                send(piece(buf, row, d), piece(kg, row, d), kgr, (s - 1, t), cond)
-
+    def piece(ref, row, d):
+        return ref.at[row, chunk((z + 8 - d) % 8)]
+
+    def pass_on(buf, row, d, recv, dev):
+        send(piece(buf, row, d), piece(buf, row, d), recv, dev, second)
+
+    def hand_over(row, d):
+        send(piece(AG, row, d), piece(kg, row, d), kgr, (s - 1, t), second)
+
+    def along_z(buf, azr):
         for d in (4, 3, 5, 2, 6, 1, 7):
-            pass_on(x, 0, azr.at[d], (s, x * 8 + (z + d) % 8))
+            pass_on(buf, x, 0, azr.at[d], (s, x * 8 + (z + d) % 8))
+
+    def along_x(buf, azr, axr):
         for d in order:
             if d:
-                arrive_if(cond, piece(buf, x, d), azr.at[d])
-            pass_on(x, d, axr.at[0, d], (s, right * 8 + z))
-            pass_on(x, d, axr.at[1, d], (s, left * 8 + z))
+                arrive_if(second, piece(buf, x, d), azr.at[d])
+            pass_on(buf, x, d, axr.at[0, d], (s, right * 8 + z))
+            pass_on(buf, x, d, axr.at[1, d], (s, left * 8 + z))
+
+    def further_x(buf, axr):
         for at, d in enumerate(order):
-            arrive_if(cond, piece(buf, left, d), axr.at[0, d])
-            arrive_if(cond, piece(buf, right, d), axr.at[1, d])
+            arrive_if(second, piece(buf, left, d), axr.at[0, d])
+            arrive_if(second, piece(buf, right, d), axr.at[1, d])
             if at % 2:
-                pass_on(left, d, axr.at[2, d], (s, right * 8 + z))
+                pass_on(buf, left, d, axr.at[2, d], (s, right * 8 + z))
             else:
-                pass_on(right, d, axr.at[2, d], (s, left * 8 + z))
-            hand_over(x, d)
+                pass_on(buf, right, d, axr.at[2, d], (s, left * 8 + z))
+
+    working = s > 0
+    mine = kg.at[x, chunk(z)]
+    own_sum = AG.at[x, chunk(z)]
+    reduce_terms(working, PX, GL, RS, RL, pxr, glr, rsr, own_sum)
+    send(own_sum, mine, chr, (s - 1, t), lower)
+    along_z(AG, azr)
+    reduce_terms(top, PX2, GL2, RS2, RL2, px2r, gl2r, rs2r, mine)
+    arrive_if(forward, mine, chr)
+    along_z(kg, az2r)
+    along_x(AG, azr, axr)
+    along_x(kg, az2r, ax2r)
+    further_x(AG, axr)
+    further_x(kg, ax2r)
+    for row in (x, left, right):
         for d in order:
-            hand_over(left, d)
-            hand_over(right, d)
-        for d in order:
-            arrive_if(cond, piece(buf, far, d), axr.at[2, d])
-            hand_over(far, d)
-
-    working = s > 0
-    reduce_terms(working, PX, GL, RS, RL, pxr, glr, rsr, AG.at[x, chunk(z)])
-    gather_sum(working, AG, azr, axr, True)
-    reduce_terms(top, PX2, GL2, RS2, RL2, px2r, gl2r, rs2r, kg.at[x, chunk(z)])
-    gather_sum(top, kg, az2r, ax2r, False)
-    arrive_if(s < 2 * PLANES - 1, kg, kgr)
+            hand_over(row, d)
+    for d in order:
+        arrive_if(second, piece(AG, far, d), axr.at[2, d])
+        hand_over(far, d)
+    for d in order:
+        arrive_if(second, piece(kg, far, d), ax2r.at[2, d])
+    arrive_if(first, kg, kgr)
     for mm in range(2):
         arrive(act.at[mm], acr.at[mm])
         arrive(grad.at[mm], grr.at[mm])
@@ -517,11 +560,11 @@
             pltpu.VMEM((4, 128, 128), F32),
             pltpu.VMEM((4, 128, 128), F32),
             pltpu.VMEM((2, 128, 128), F32),
-            weight, weight, weight, weight, frame(4), pltpu.VMEM((4, 8 * ROWS, 128), BF16),
+            frame(8), weight, weight, weight, weight, frame(4), pltpu.VMEM((4, 8 * ROWS, 128), BF16),
             *terms, *terms,
-            dma((210,)), dma, dma((4,)), dma((3,)), dma, dma, dma((2,)), dma((2,)),
+            dma((220,)), dma, dma((4,)), dma((3,)), dma, dma, dma((2,)), dma((2,)),
             dma((4,)), dma((4,)), dma((8,)), dma((4,)), dma((4,)), dma((8,)),
-            dma, dma((8,)), dma((3, 8)), dma((8,)), dma((3, 8)),
+            dma, dma, dma((8,)), dma((3, 8)), dma((8,)), dma((3, 8)),
         ],
         compiler_params=pltpu.CompilerParams(
             collective_id=0, has_side_effects=True, vmem_limit_bytes=48 << 20,

time: 141 us -> 130 us (0.922)
  Pallas kernels: 134 us -> 124 us
    pallas_call x1, Pallas kernels: 134 us -> 124 us  [body(): pl.pallas_call(kernel, out_shape=(jax.ShapeDtypeStruct((2, 128, 128), BF1...]
where the time goes in v3:
time: 130 us
  Pallas kernels  124 us (95%)
  local copies, waits for them, and re-layouts  5.48 us (4%)
    pallas_call x1, Pallas kernels, body(): pl.pallas_call(kernel, out_shape=(jax.ShapeDtypeStruct((2, 128, 128), BF1...  124 us
    unnamed x8, local copies, waits for them, and re-layouts  4.1 us

profile of v3, /device:TPU:1, one launch (start us, length us, event | category | flops | bytes accessed | tf_op | source)
XLA Modules:
  0.0 130.2 jit_solution(13169054374575571334)
XLA Ops:
  0.6 0.0 copy-start
  0.6 1.2 copy-done
  1.8 0.0 copy-start.1
  1.8 0.8 copy-done.1
  2.6 0.0 copy-start.2
  2.6 0.8 copy-done.2
  3.5 123.9 %blocks.1 = (bf16[2,128,128]{2,1,0:T(8,128)(2,1)S(1)}, bf16[2,128,128]{2,1,0:T(8,128)(2,1)S(1)}, bf16[4,896,128]{2,1,0:T(8,128)(2,1)S(1)}) custom-call(bf16[2,128,128]{2,1,0:T(8,128)(2,1)S(1)} %bitcast.14, bf16[27,128,128]{2,1,0:T(8,128)(2,1)S(1)} %bitcast.13, bf16[2,128,128]{2,1,0:T(8,128)(2,1)S(1)} %bitcast.15), custom_call_target="tpu_custom_call" | custom-call | tf_op jit(solution)/shard_map/blocks/pallas_call | solution.py:549
  127.4 0.1 convert_multiply_fusion
  127.5 1.4 %copy.6 = f32[27,4,32,128]{3,2,1,0:T(8,128)} copy(f32[27,4,32,128]{3,2,0,1:T(8,128)S(1)} %bitcast.18) | data formatting | bytes 3538944 | tf_op jit(solution)/shard_map/mul | solution.py:580
  128.9 0.6 copy.11
  129.5 0.6 copy.12
Async XLA Ops:
  0.6 1.2 copy-start
  1.8 0.8 copy-start.1
  2.6 0.8 copy-start.2

commit v4 on v3

--- a/solution.py
+++ b/solution.py
@@ -9,7 +9,7 @@
 
 MESH = pl.DeviceIdType.MESH
 PLANES = 8
-ROWS = 112
+CLIP_PLANE = {2: 0, 1: 0, 0: 0, -1: 0}
 BF16 = jnp.bfloat16
 F32 = jnp.float32
 
@@ -61,10 +61,10 @@
 
 
 def kernel(
-    clips, k_hbm, cot, act, grad, kg,
-    X0, X1, X2, G2, G1, G0, BK, S1, S0, SX, WfA, WfB, WbA, WbB, KX, AG,
+    clips_hbm, k_hbm, cot, act, grad, kg,
+    X0, X1, X2, G2, G1, G0, BK, S1, S0, SX, clips, WfA, WfB, WbA, WbB, KX, AG, CH,
     TT, PX, GL, RS, RL, TT2, PX2, GL2, RS2, RL2,
-    SS, ownr, x0r, g2r, kr, kxr, acr, grr, pxr, glr, rsr, px2r, gl2r, rs2r, kgr, chr, azr, axr, az2r, ax2r,
+    SS, ownr, clr, x0r, g2r, kr, kxr, acr, grr, pxr, glr, rsr, px2r, gl2r, rs2r, kgr, chr, evr, azr, axr, az2r, ax2r,
 ):
     s = lax.axis_index("section")
     t = lax.axis_index("tm")
@@ -116,6 +116,8 @@
         dt, n = tap // 9, tap % 9
         return ref.at[dt * 128 : (dt + 1) * 128, n * 128 : (n + 1) * 128]
 
+    base = both(second, y == 0)
+    pl.when(base)(lambda: pltpu.make_async_copy(clips_hbm, clips, clr).start())
     entry = pltpu.get_barrier_semaphore()
     expected = []
 
@@ -125,14 +127,20 @@
     def expect(cond):
         expected.append(cond.astype(jnp.int32))
 
+    always = s >= 0
+    for d in (4, 3, 5, 2, 6, 1, 7):
+        greet(always, (s, x * 8 + (z + d) % 8))
+        expect(always)
     inside = lambda v, top: both(v >= 0, v <= top)
     for k in range(-4, 4):
         at = 2 * j + k
-        greet(both(both(second, y == 0), both(inside(at, 31), at != t)), (1, at))
+        plane = CLIP_PLANE[-(k // 2)]
+        away = at != t if plane == 0 else always
+        greet(both(both(second, y == 0), both(inside(at, 31), away)), (2 * plane + 1, at))
     for dj in (2, 1, 0, -1):
         for mm in range(2):
-            ok = both(both(second, y == 0), inside(q + dj, 15))
-            expect(both(ok, tm_of(mm, q + dj) != t))
+            away = tm_of(mm, q + dj) != t if CLIP_PLANE[dj] == 0 else always
+            expect(both(both(second, y == CLIP_PLANE[dj]), both(inside(q + dj, 15), away)))
     for dj in (2, 1, 0, -1):
         greet(both(both(second, y > 0), inside(j - dj, 15)), (s - 2, tm_of(m, j - dj)))
         expect(both(both(second, y < PLANES - 1), inside(j + dj, 15)))
@@ -145,21 +153,13 @@
     for dj in (0, -1, -2):
         for mm in range(2):
             expect(both(both(first, y == PLANES - 1), inside(q + dj, 15)))
-    always = s >= 0
     for d in range(4):
         greet(first, (s + 1, (x + d) % 4 * 8 + z))
         expect(second)
     greet(second, (s - 1, t))
     expect(first)
-    greet(both(first, y > 0), (s - 1, t))
-    expect(both(second, y < PLANES - 1))
-    greet(both(second, y < PLANES - 1), (s + 1, t))
-    expect(both(first, y > 0))
     for d in range(1, 4):
         greet(always, (s, (x + d) % 4 * 8 + z))
-        expect(always)
-    for d in range(1, 8):
-        greet(always, (s, x * 8 + (z + d) % 8))
         expect(always)
     for mm in range(2):
         at = tm_of(mm, q)
@@ -174,14 +174,18 @@
 
     pl.semaphore_wait(entry, sum(expected))
 
+    pl.when(base)(lambda: pltpu.make_async_copy(clips_hbm, clips, clr).wait())
+
     for dj in (2, 1, 0, -1):
         for mm in range(2):
             there = q + dj
-            ok = both(both(second, y == 0), both(there >= 0, there <= 15))
+            ok = both(both(second, y == CLIP_PLANE[dj]), inside(there, 15))
             to = tm_of(mm, there)
-            send_or_copy(
-                clips.at[mm], X0.at[(2 - dj) * 2 + e], x0r.at[2 - dj], (1, to), ok, to == t
-            )
+            slot = (2 - dj) * 2 + e
+            if CLIP_PLANE[dj] == 0:
+                send_or_copy(clips.at[mm], X0.at[slot], x0r.at[2 - dj], (1, to), ok, to == t)
+            else:
+                send(clips.at[mm], X0.at[slot], x0r.at[2 - dj], (1, to), ok)
     idx = len(drains)
     all_taps = lambda: remote(k_hbm, k_hbm, kr, (s + 1, t), idx)
     drains.append((first, all_taps))
@@ -268,7 +272,7 @@
         pltpu.make_async_copy(WfB, WfB, ownr).wait()
         arrive(WfA, kr)
 
-        @pl.when(y > 0)
+        @pl.when(y > 2)
         def _():
             bwd_weight(WbB, WfB)
             bwd_weight(WbA, WfA)
@@ -330,7 +334,7 @@
 
     top = both(second, y == PLANES - 1)
 
-    @pl.when(both(second, y == 0))
+    @pl.when(both(second, y <= 2))
     def _():
         bwd_weight(WbB, WfB)
         bwd_weight(WbA, WfA)
@@ -342,7 +346,11 @@
         block_a(4, 6)
 
     flush()
-    send(X1.at[0:4], KX, kxr, (s + 1, t), forward)
+    behind = both(second, y > 0)
+    lower = both(first, y > 0)
+    ground = both(second, y == 0)
+    send(X1.at[0:4], KX, kxr, (s + 2, t), forward)
+    send(X0.at[2:6], KX, kxr, (s - 1, t), behind)
 
     def swap_patches(cond, TT, PX, pxr):
         for d in range(4):
@@ -353,9 +361,14 @@
             else:
                 send(src, PX.at[x], pxr.at[d], (s, other * 8 + z), cond)
 
-    @pl.when(forward)
+    @pl.when(ground)
     def _():
         build_patches(X0.at[2:6], TT)
+
+    @pl.when(both(forward, y > 0))
+    def _():
+        arrive(KX, kxr)
+        build_patches(KX, TT)
 
     swap_patches(forward, TT, PX, pxr)
     out_home(X1.at[2:4], act, acr, 0, forward)
@@ -389,7 +402,7 @@
             send(src, GL.at[x], glr.at[d], (s, other * 8 + z), cond)
         pl.when(cond)(lambda: pltpu.make_async_copy(src, GL.at[x], glr.at[0]).start())
 
-    gather(G1.at[0:2], GL, glr, both(second, y == 0))
+    gather(G1.at[0:2], GL, glr, ground)
 
     @pl.when(second)
     def _():
@@ -404,14 +417,13 @@
             ok = both(ok, when)
         send_fast(G0, G2.at[-2 * dj : -2 * dj + 2], g2r.at[-dj], (s - 2, tm_of(m, there)), ok)
     flush()
-    behind = both(second, y > 0)
+    gather(G0, GL, glr, behind)
     for d in (2, 1, 3, 0):
         other = (x + d) % 4
-        send(G0, GL.at[x], glr.at[d], (s - 1, other * 8 + z), behind)
-    gather(G1.at[0:2], GL, glr, behind)
+        send(G1.at[0:2], GL.at[x], glr.at[d], (s - 1, other * 8 + z), behind)
     gather(G2.at[0:2], GL2, gl2r, top)
-    out_home(G0, grad, grr, 0, second)
-    out_home(G1, grad, grr, 1, second)
+    out_home(G0, grad, grr, 0, behind)
+    out_home(G1, grad, grr, 1, behind)
 
     @pl.when(top)
     def _():
@@ -419,26 +431,23 @@
         take(0)
         block_a(0, 2)
         block_b()
-        build_patches(X0.at[2:6], TT)
         build_patches(X1, TT2)
 
     out_home(X1.at[2:4], act, acr, 0, top)
     out_home(X2, act, acr, 1, top)
     swap_patches(top, TT2, PX2, px2r)
 
-    lower = both(first, y > 0)
-
-    @pl.when(lower)
+    @pl.when(jnp.logical_or(lower, top))
     def _():
         arrive(KX, kxr)
         build_patches(KX, TT)
 
     swap_patches(jnp.logical_or(lower, top), TT, PX, pxr)
 
-    def chunk(k):
-        return pl.ds(pl.multiple_of(k * ROWS, 16), ROWS)
-
-    def reduce_terms(cond, PX, GL, RS, RL, pxr, glr, rsr, out):
+    def taps_of(k):
+        return pl.ds(7 * (k % 4), 7)
+
+    def reduce_terms(cond, PX, GL, RS, RL, pxr, glr, rsr, out, between=lambda: None):
         @pl.when(cond)
         def _():
             for d in range(4):
@@ -453,16 +462,17 @@
                     )
                     term = jnp.dot(left, GL[p].reshape(256, 128), preferred_element_type=F32)
                     total = term if total is None else total + term
-                RS[dt * 288 : (dt + 1) * 288, :] = total.astype(BF16)
-            RS[864:896, :] = jnp.zeros((32, 128), BF16)
+                RS[dt * 9 : (dt + 1) * 9] = total.astype(BF16).reshape(9, 2, 16, 128)
+            RS[27] = jnp.zeros((2, 16, 128), BF16)
 
         for d in (4, 3, 5, 2, 6, 1, 7):
             other = (z + d) % 8
-            send(RS.at[chunk(other)], RL.at[z], rsr.at[d], (s, x * 8 + other), cond)
+            send(RS.at[taps_of(other), other // 4], RL.at[z], rsr.at[d], (s, x * 8 + other), cond)
+        between()
 
         @pl.when(cond)
         def _():
-            total = RS[chunk(z), :].astype(F32)
+            total = RS[taps_of(z), z // 4].astype(F32)
             for d in range(1, 8):
                 source = (z + 8 - d) % 8
                 arrive(RL.at[source], rsr.at[d])
@@ -473,7 +483,8 @@
     order = (0, 1, 7, 2, 6, 3, 5, 4)
 
     def piece(ref, row, d):
-        return ref.at[row, chunk((z + 8 - d) % 8)]
+        k = (z + 8 - d) % 8
+        return ref.at[taps_of(k), 2 * row + k // 4]
 
     def pass_on(buf, row, d, recv, dev):
         send(piece(buf, row, d), piece(buf, row, d), recv, dev, second)
@@ -501,11 +512,21 @@
             else:
                 pass_on(buf, right, d, axr.at[2, d], (s, left * 8 + z))
 
-    working = s > 0
-    mine = kg.at[x, chunk(z)]
-    own_sum = AG.at[x, chunk(z)]
-    reduce_terms(working, PX, GL, RS, RL, pxr, glr, rsr, own_sum)
-    send(own_sum, mine, chr, (s - 1, t), lower)
+    mine = piece(kg, x, 0)
+    even_sum = piece(AG, x, 0)
+    def last_home():
+        out_home(G0, grad, grr, 0, ground)
+        out_home(G1, grad, grr, 1, ground)
+
+    reduce_terms(s > 0, PX, GL, RS, RL, pxr, glr, rsr, CH, last_home)
+    send(CH, mine, chr, (s - 2, t), behind)
+    send(CH, even_sum, evr, (s + 1, t), lower)
+
+    @pl.when(ground)
+    def _():
+        even_sum[...] = CH[...]
+
+    arrive_if(behind, even_sum, evr)
     along_z(AG, azr)
     reduce_terms(top, PX2, GL2, RS2, RL2, px2r, gl2r, rs2r, mine)
     arrive_if(forward, mine, chr)
@@ -543,31 +564,31 @@
         pltpu.VMEM((4, 9, 128, 128), BF16),
         pltpu.VMEM((4, 4, 9, 32, 128), BF16),
         pltpu.VMEM((4, 2, 128, 128), BF16),
-        pltpu.VMEM((8 * ROWS, 128), BF16),
-        pltpu.VMEM((8, ROWS, 128), BF16),
+        pltpu.VMEM((28, 2, 16, 128), BF16),
+        pltpu.VMEM((8, 7, 16, 128), BF16),
     )
     act, grad, kg = pl.pallas_call(
         kernel,
         out_shape=(
             jax.ShapeDtypeStruct((2, 128, 128), BF16),
             jax.ShapeDtypeStruct((2, 128, 128), BF16),
-            jax.ShapeDtypeStruct((4, 8 * ROWS, 128), BF16),
+            jax.ShapeDtypeStruct((28, 8, 16, 128), BF16),
         ),
-        in_specs=[pl.BlockSpec(memory_space=pl.ANY)] * 3,
+        in_specs=[pl.BlockSpec(memory_space=pltpu.HBM)] * 3,
         out_specs=(vmem,) * 3,
         scratch_shapes=[
             frame(8), frame(6), frame(2), frame(6), frame(4), frame(2),
             pltpu.VMEM((4, 128, 128), F32),
             pltpu.VMEM((4, 128, 128), F32),
             pltpu.VMEM((2, 128, 128), F32),
-            frame(8), weight, weight, weight, weight, frame(4), pltpu.VMEM((4, 8 * ROWS, 128), BF16),
+            frame(8), frame(2), weight, weight, weight, weight, frame(4), pltpu.VMEM((28, 8, 16, 128), BF16), pltpu.VMEM((7, 16, 128), BF16),
             *terms, *terms,
-            dma((220,)), dma, dma((4,)), dma((3,)), dma, dma, dma((2,)), dma((2,)),
+            dma((220,)), dma, dma, dma((4,)), dma((3,)), dma, dma, dma((2,)), dma((2,)),
             dma((4,)), dma((4,)), dma((8,)), dma((4,)), dma((4,)), dma((8,)),
-            dma, dma, dma((8,)), dma((3, 8)), dma((8,)), dma((3, 8)),
+            dma, dma, dma, dma((8,)), dma((3, 8)), dma((8,)), dma((3, 8)),
         ],
         compiler_params=pltpu.CompilerParams(
-            collective_id=0, has_side_effects=True, vmem_limit_bytes=48 << 20,
+            collective_id=0, has_side_effects=True, vmem_limit_bytes=60 << 20,
         ),
         name="blocks",
     )(
@@ -577,7 +598,7 @@
     )
     total = micro * frames * lax.axis_size("tm") * height * width
     norm = 1.0 / jnp.sqrt(jnp.float32(total))
-    parts = kg[:, :864].reshape(4, 27, 32, 128).transpose(1, 0, 2, 3).astype(F32) * norm
+    parts = kg[:27].reshape(27, chan, chan).astype(F32) * norm
     return (
         act.reshape(1, micro, 1, height, width, chan),
         grad.reshape(1, micro, 1, height, width, chan),

time: 130 us -> 129 us (level)
  local copies, waits for them, and re-layouts: 5.48 us -> 1.27 us
  other arithmetic: 0.14 us -> 2.63 us
    unnamed x8 -> x6, local copies, waits for them, and re-layouts: 4.1 us -> 1.27 us
    mul x1, other arithmetic: 0.14 us -> 2.63 us  [body(): parts = kg[:27].reshape(27, chan, chan).astype(F32) * norm]
    mul x1 -> x0, local copies, waits for them, and re-layouts: 1.38 us -> none  [body(): kg[:, :864].reshape(4, 27, 32, 128).transpose(1, 0, 2, 3).astype(F32) * norm]
where the time goes in v4:
time: 129 us
  Pallas kernels  125 us (97%)
  other arithmetic  2.63 us (2%)
    pallas_call x1, Pallas kernels, body(): pl.pallas_call(kernel, out_shape=(jax.ShapeDtypeStruct((2, 128, 128), BF1...  125 us
    mul x1, other arithmetic, body(): parts = kg[:27].reshape(27, chan, chan).astype(F32) * norm  2.63 us

profile of v4, /device:TPU:1, one launch (start us, length us, event | category | flops | bytes accessed | tf_op | source)
XLA Modules:
  0.0 129.4 jit_solution(16276281641205247018)
XLA Ops:
  0.6 124.8 %blocks.1 = (bf16[2,128,128]{2,1,0:T(8,128)(2,1)}, bf16[2,128,128]{2,1,0:T(8,128)(2,1)}, bf16[28,8,16,128]{3,2,1,0:T(8,128)(2,1)}) custom-call(bf16[2,128,128]{2,1,0:T(8,128)(2,1)} %bitcast.12, bf16[27,128,128]{2,1,0:T(8,128)(2,1)} %bitcast.11, bf16[2,128,128]{2,1,0:T(8,128)(2,1)} %bitcast.13), custom_call_target="tpu_custom_call" | custom-call | tf_op jit(solution)/shard_map/blocks/pallas_call | solution.py:570
  125.4 0.0 copy-start.1
  125.4 0.0 copy-start
  125.5 2.6 %convert_multiply_fusion = f32[27,8,16,128]{3,2,1,0:T(8,128)} fusion(bf16[28,8,16,128]{3,2,1,0:T(8,128)(2,1)} %get-tuple-element.8), kind=kLoop, calls=%fused_computation | loop fusion | flops 884736 | bytes 2654208 | tf_op jit(solution)/shard_map/mul | solution.py:601
  128.1 0.0 copy-done.1
  128.1 0.6 copy.10
  128.7 0.0 copy-done
  128.7 0.6 copy.11
Async XLA Ops:
  125.4 2.7 %copy-start.1 = (bf16[2,128,128]{2,1,0:T(8,128)(2,1)S(1)}, bf16[2,128,128]{2,1,0:T(8,128)(2,1)}, u32[]{:S(2)}) copy-start(bf16[2,128,128]{2,1,0:T(8,128)(2,1)} %get-tuple-element.6) | copy-start | bytes 196612
  125.4 3.3 %copy-start = (bf16[2,128,128]{2,1,0:T(8,128)(2,1)S(1)}, bf16[2,128,128]{2,1,0:T(8,128)(2,1)}, u32[]{:S(2)}) copy-start(bf16[2,128,128]{2,1,0:T(8,128)(2,1)} %get-tuple-element.7) | copy-start | bytes 196612

commit v5 on v4

--- a/solution.py
+++ b/solution.py
@@ -62,7 +62,7 @@
 
 def kernel(
     clips_hbm, k_hbm, cot, act, grad, kg,
-    X0, X1, X2, G2, G1, G0, BK, S1, S0, SX, clips, WfA, WfB, WbA, WbB, KX, AG, CH,
+    X0, X1, X2, G2, G1, G0, BK, S1, S0, SX, SB, clips, WfA, WfB, WbA, WbB, KX, AG, CH,
     TT, PX, GL, RS, RL, TT2, PX2, GL2, RS2, RL2,
     SS, ownr, clr, x0r, g2r, kr, kxr, acr, grr, pxr, glr, rsr, px2r, gl2r, rs2r, kgr, chr, evr, azr, axr, az2r, ax2r,
 ):
@@ -227,10 +227,13 @@
     def block_a(lo, hi):
         out = conv([SX[k] for k in range(lo, hi + 2)], WfA)
         for k in range(lo, hi):
-            X1[k] = (X0[k + 2].astype(F32) + out[k - lo]).astype(BF16)
+            v = (X0[k + 2].astype(F32) + out[k - lo]).astype(BF16)
+            X1[k] = v
+            if k < 4:
+                SB[k] = silu(v.astype(F32)).astype(BF16)
 
     def block_b():
-        out = conv([frame_silu(X1, k) for k in range(4)], WfB)
+        out = conv([SB[k] for k in range(4)], WfB)
         for k in range(2):
             X2[k] = (X1[k + 2].astype(F32) + out[k]).astype(BF16)
 
@@ -581,7 +584,7 @@
             pltpu.VMEM((4, 128, 128), F32),
             pltpu.VMEM((4, 128, 128), F32),
             pltpu.VMEM((2, 128, 128), F32),
-            frame(8), frame(2), weight, weight, weight, weight, frame(4), pltpu.VMEM((28, 8, 16, 128), BF16), pltpu.VMEM((7, 16, 128), BF16),
+            frame(8), frame(4), frame(2), weight, weight, weight, weight, frame(4), pltpu.VMEM((28, 8, 16, 128), BF16), pltpu.VMEM((7, 16, 128), BF16),
             *terms, *terms,
             dma((220,)), dma, dma, dma((4,)), dma((3,)), dma, dma, dma((2,)), dma((2,)),
             dma((4,)), dma((4,)), dma((8,)), dma((4,)), dma((4,)), dma((8,)),

time: 129 us -> 130 us (level)
  no operation moved by 1% of the time
where the time goes in v5:
time: 130 us
  Pallas kernels  125 us (96%)
  other arithmetic  2.63 us (2%)
    pallas_call x1, Pallas kernels, body(): pl.pallas_call(kernel, out_shape=(jax.ShapeDtypeStruct((2, 128, 128), BF1...  125 us
    mul x1, other arithmetic, body(): parts = kg[:27].reshape(27, chan, chan).astype(F32) * norm  2.63 us

profile of v5, /device:TPU:1, one launch (start us, length us, event | category | flops | bytes accessed | tf_op | source)
XLA Modules:
  0.0 129.8 jit_solution(14646772496854412651)
XLA Ops:
  0.6 125.2 %blocks.1 = (bf16[2,128,128]{2,1,0:T(8,128)(2,1)}, bf16[2,128,128]{2,1,0:T(8,128)(2,1)}, bf16[28,8,16,128]{3,2,1,0:T(8,128)(2,1)}) custom-call(bf16[2,128,128]{2,1,0:T(8,128)(2,1)} %bitcast.12, bf16[27,128,128]{2,1,0:T(8,128)(2,1)} %bitcast.11, bf16[2,128,128]{2,1,0:T(8,128)(2,1)} %bitcast.13), custom_call_target="tpu_custom_call" | custom-call | tf_op jit(solution)/shard_map/blocks/pallas_call | solution.py:573
  125.9 0.0 copy-start.1
  125.9 0.0 copy-start
  125.9 2.6 %convert_multiply_fusion = f32[27,8,16,128]{3,2,1,0:T(8,128)} fusion(bf16[28,8,16,128]{3,2,1,0:T(8,128)(2,1)} %get-tuple-element.8), kind=kLoop, calls=%fused_computation | loop fusion | flops 884736 | bytes 2654208 | tf_op jit(solution)/shard_map/mul | solution.py:604
  128.5 0.0 copy-done.1
  128.5 0.6 copy.10
  129.1 0.0 copy-done
  129.1 0.6 copy.11
Async XLA Ops:
  125.9 2.7 %copy-start.1 = (bf16[2,128,128]{2,1,0:T(8,128)(2,1)S(1)}, bf16[2,128,128]{2,1,0:T(8,128)(2,1)}, u32[]{:S(2)}) copy-start(bf16[2,128,128]{2,1,0:T(8,128)(2,1)} %get-tuple-element.6) | copy-start | bytes 196612
  125.9 3.3 %copy-start = (bf16[2,128,128]{2,1,0:T(8,128)(2,1)S(1)}, bf16[2,128,128]{2,1,0:T(8,128)(2,1)}, u32[]{:S(2)}) copy-start(bf16[2,128,128]{2,1,0:T(8,128)(2,1)} %get-tuple-element.7) | copy-start | bytes 196612
